TPU v7x, 512 devices: a whole 4x4x16 slice. The times are simulated.
512 devices in a mesh: row: 16 (over x, y_lo, core), col: 32 (over z, y_hi).
Axes of the slice: x: 4, y: 4 (y_hi: 2, y_lo: 2; y = y_hi * 2 + y_lo), z: 16, core: 2. Of those that a mesh axis runs over, the one named last changes fastest.
Arguments:
- features: bfloat16 [128, 1024, 256], P('row', 'col'), may hold values from -16 to 16
- expand_weight: bfloat16 [2, 256, 1024], replicated, may hold values from -0.375 to 0.375
- expand_bias: float32 [2, 1024], replicated, may hold values from -3 to 3
- depth_weight: float32 [2, 3, 3, 1024], replicated, may hold values from -2 to 2
- depth_bias: float32 [2, 1024], replicated, may hold values from -3 to 3
- project_weight: bfloat16 [2, 1024, 256], replicated, may hold values from -0.1875 to 0.1875
- project_bias: float32 [2, 256], replicated, may hold values from -3 to 3
- qkv_weight: bfloat16 [2, 256, 768], replicated, may hold values from -0.375 to 0.375
- aggregate_depth: float32 [2, 5, 5, 768], replicated, may hold values from -1.25 to 1.25
- aggregate_group: bfloat16 [2, 24, 32, 32], replicated, may hold values from -1 to 1
- output_weight: bfloat16 [2, 512, 256], replicated, may hold values from -0.25 to 0.25
- output_bias: float32 [2, 256], replicated, may hold values from -3 to 3
- head_weight: bfloat16 [3, 3, 4, 256], replicated, may hold values from -0.125 to 0.125
- head_bias: float32 [4], replicated, may hold values from -3 to 3
Outputs:
- final_map: bfloat16 [128, 1024, 256], P('row', 'col')
- boxes: float32 [4, 128, 1024], P(None, 'row', 'col')
All inputs are finite; a program needn't handle non-finite values.
Results may differ from a plain program's by a relative error of at most 0.009.
Values may be sent and summed in bfloat16 or wider, within the bound.
A program may use at most 64 MiB of HBM per device.

v0:
```python
import jax
import jax.numpy as jnp
from jax import lax
from jax.sharding import PartitionSpec as P

SECTIONS = 2


def with_halo(cells, sides, width):
    for axis, dim in sides:
        count = lax.axis_size(axis)
        ends = count - 1
        head = lax.slice_in_dim(cells, 0, width, axis=dim)
        tail = lax.slice_in_dim(cells, cells.shape[dim] - width, cells.shape[dim], axis=dim)
        cells = jnp.concatenate(
            [
                lax.ppermute(tail, axis, [(i, (i + 1) % count) for i in range(ends)]),
                cells,
                lax.ppermute(head, axis, [((i + 1) % count, i) for i in range(ends)]),
            ],
            axis=dim,
        )
    return cells


def hard_swish(value):
    return value * jnp.minimum(jnp.maximum(value + 3.0, 0.0), 6.0) / 6.0


def depthwise(padded, weight, rows, cols):
    ksize = weight.shape[0]
    total = jnp.zeros((rows, cols, padded.shape[2]), jnp.float32)
    for offset_r in range(ksize):
        for offset_c in range(ksize):
            total = (
                total
                + padded[offset_r : offset_r + rows, offset_c : offset_c + cols, :].astype(
                    jnp.float32
                )
                * weight[offset_r, offset_c]
            )
    return total


def dense(values, weight):
    return lax.dot_general(
        values, weight, (((values.ndim - 1,), (0,)), ((), ())), preferred_element_type=jnp.float32
    )


def heads_of(padded_qkv, agg_depth, agg_group, rows, cols, heads, head_dim):
    center = padded_qkv[2 : 2 + rows, 2 : 2 + cols, :]
    spread = depthwise(padded_qkv, agg_depth, rows, cols).astype(jnp.bfloat16)
    grouped = jnp.einsum(
        "rcgd,gde->rcge",
        spread.reshape(rows, cols, 3 * heads, head_dim),
        agg_group,
        preferred_element_type=jnp.float32,
    ).astype(jnp.bfloat16)
    return jnp.concatenate(
        [
            center.reshape(rows, cols, heads, 3, head_dim),
            grouped.reshape(rows, cols, heads, 3, head_dim),
        ],
        axis=2,
    )


def local(
    features,
    expand_weight,
    expand_bias,
    depth_weight,
    depth_bias,
    project_weight,
    project_bias,
    qkv_weight,
    aggregate_depth,
    aggregate_group,
    output_weight,
    output_bias,
    head_weight,
    head_bias,
):
    rows, cols, width = features.shape
    head_dim = aggregate_group.shape[2]
    heads = width // head_dim
    current = features
    for section in range(SECTIONS):
        hidden = hard_swish(dense(current, expand_weight[section]) + expand_bias[section]).astype(
            jnp.bfloat16
        )
        hidden = with_halo(hidden, (("row", 0), ("col", 1)), 1)
        spread = hard_swish(
            depthwise(hidden, depth_weight[section], rows, cols) + depth_bias[section]
        ).astype(jnp.bfloat16)
        mixed = (current + dense(spread, project_weight[section]) + project_bias[section]).astype(
            jnp.bfloat16
        )
        local_qkv = dense(mixed, qkv_weight[section]).astype(jnp.bfloat16)
        padded_qkv = with_halo(local_qkv, (("row", 0), ("col", 1)), 2)
        both = heads_of(
            padded_qkv,
            aggregate_depth[section],
            aggregate_group[section],
            rows,
            cols,
            heads,
            head_dim,
        )
        queries = jax.nn.relu(both[:, :, :, 0, :]).astype(jnp.float32)
        keys = jax.nn.relu(both[:, :, :, 1, :]).astype(jnp.float32)
        values = both[:, :, :, 2, :].astype(jnp.float32)
        kv_local = jnp.einsum("rchd,rche->hde", keys, values, precision=lax.Precision.HIGHEST)
        key_local = jnp.sum(keys, axis=(0, 1))
        kv_all, key_all = lax.psum((kv_local, key_local), ("row", "col"))
        numer = jnp.einsum("rchd,hde->rche", queries, kv_all, precision=lax.Precision.HIGHEST)
        denom = jnp.einsum("rchd,hd->rch", queries, key_all, precision=lax.Precision.HIGHEST)
        attended = (
            (numer / (denom[..., None] + 1e-06)).astype(jnp.bfloat16).reshape(rows, cols, 2 * width)
        )
        current = (mixed + dense(attended, output_weight[section]) + output_bias[section]).astype(
            jnp.bfloat16
        )
    padded = with_halo(current, (("row", 0), ("col", 1)), 1)
    boxes = jnp.zeros((4, rows, cols), jnp.float32)
    for offset_r in range(3):
        for offset_c in range(3):
            window = padded[offset_r : offset_r + rows, offset_c : offset_c + cols, :]
            boxes = boxes + lax.dot_general(
                head_weight[offset_r, offset_c],
                window,
                (((1,), (2,)), ((), ())),
                preferred_element_type=jnp.float32,
            )
    boxes = boxes + head_bias[:, None, None]
    return (current, boxes)


def solution(mesh):
    return jax.shard_map(
        local,
        mesh=mesh,
        in_specs=(
            P("row", "col", None),
            P(),
            P(),
            P(),
            P(),
            P(),
            P(),
            P(),
            P(),
            P(),
            P(),
            P(),
            P(),
            P(),
        ),
        out_specs=(P("row", "col", None), P(None, "row", "col")),
        check_vma=False,
    )
```

profile of v0, /device:TPU:1, one launch (start us, length us, event | category | flops | bytes accessed | tf_op | source)
XLA Modules:
  0.0 1291.3 jit_solution(16654592046291332820)
XLA Ops:
  7.3 1.4 fusion.129
  8.6 1.5 multiply_convert_fusion.3
  10.1 4.6 collective-permute-start
  14.7 5.5 collective-permute-start.1
  21.7 0.7 copy_bitcast_fusion
  23.1 1.9 collective-permute-start.2
  24.9 1.3 collective-permute-start.3
  26.2 0.7 slice_reduce_fusion.49
  27.0 4.2 collective-permute-done.3
  31.6 1.5 fusion.11
  33.4 0.7 fusion.122
  34.1 3.7 collective-permute-start.4
  37.8 1.9 collective-permute-start.5
  39.7 0.6 slice_reduce_fusion.48
  40.4 1.6 reshape.49
  42.0 2.0 collective-permute-done.5
  44.0 6.0 collective-permute-start.6
  50.0 1.3 collective-permute-start.7
  51.3 1.9 copy_dynamic-update-slice_fusion.3
  53.3 2.9 collective-permute-done.7
  56.7 3.0 add_convert_fusion.1
  59.7 1.1 reshape.50
  61.3 1.3 copy-done
  63.4 1.4 copy-done.1
  64.8 1.1 convolution_bitcast_fusion.1
  66.0 111.1 %psum.29 = f32[16,32]{1,0:T(8,128)S(1)} all-reduce(f32[16,32]{1,0:T(8,128)S(1)} %convert_reduce_fusion.1), channel_id=1, replica_groups=mesh['row'=16,'col'=32] {'row','col'}, use_global_device_ids=true, to_apply=%region_2.3 | all-reduce | flops 512 | bytes 4096 | tf_op jit(solution)/shard_map/psum | solution.py:116
  177.0 5.4 fusion.26
  182.5 450.1 %all-reduce.3.cloned.1.call-done = f32[16,32,32]{1,2,0:T(8,128)} async-done(((f32[16,32,32]{1,2,0:T(8,128)}), f32[16,32,32]{1,2,0:T(8,128)}) %all-reduce.3.cloned.1.call-update) | async-done | bytes 65552 | tf_op jit(solution)/shard_map/psum | solution.py:116
  632.6 6.1 fusion.1
  638.7 1.0 copy.25
  639.7 1.0 reshape.52
  640.8 1.2 fusion.8
  642.4 4.9 collective-permute-start.8
  647.3 1.9 collective-permute-start.9
  649.3 3.6 collective-permute-done.9
  653.0 4.5 collective-permute-start.10
  657.5 1.3 collective-permute-start.11
  658.9 4.8 collective-permute-done.11
  664.1 1.5 fusion.10
  666.0 2.7 collective-permute-start.12
  668.7 1.9 collective-permute-start.13
  670.7 1.6 reshape.53
  672.3 2.3 collective-permute-done.13
  674.7 3.1 collective-permute-start.14
  677.8 1.5 collective-permute-start.15
  679.3 1.9 copy_dynamic-update-slice_fusion.1
  681.2 2.8 collective-permute-done.15
  684.3 3.0 add_convert_fusion
  687.3 1.1 reshape.54
  689.0 1.3 copy-done.2
  691.1 1.4 copy-done.3
  692.4 1.1 convolution_bitcast_fusion
  693.6 105.8 %psum.31 = f32[16,32]{1,0:T(8,128)S(1)} all-reduce(f32[16,32]{1,0:T(8,128)S(1)} %convert_reduce_fusion), channel_id=1, replica_groups=mesh['row'=16,'col'=32] {'row','col'}, use_global_device_ids=true, to_apply=%region_5.6 | all-reduce | flops 512 | bytes 4096 | tf_op jit(solution)/shard_map/psum | solution.py:116
  799.4 5.4 fusion.29
  804.9 448.7 %all-reduce.5.cloned.1.call-done = f32[16,32,32]{1,2,0:T(8,128)} async-done(((f32[16,32,32]{1,2,0:T(8,128)}), f32[16,32,32]{1,2,0:T(8,128)}) %all-reduce.5.cloned.1.call-update) | async-done | bytes 65552 | tf_op jit(solution)/shard_map/psum | solution.py:116
  1253.6 6.1 fusion
  1259.8 1.0 copy.31
  1260.8 1.0 reshape.56
  1262.1 4.9 collective-permute-start.16
  1267.0 1.9 collective-permute-start.17
  1269.2 2.9 collective-permute-done.17
  1272.1 4.5 collective-permute-start.18
  1276.6 1.3 collective-permute-start.19
  1278.3 4.2 collective-permute-done.19
  (151 shorter events, 10.5 us)
Async XLA Ops:
  7.2 13.1 %copy-start.35 = (f32[2,256]{1,0:T(2,128)S(1)}, f32[2,256]{1,0:T(2,128)}, u32[]{:S(2)}) copy-start(f32[2,256]{1,0:T(2,128)} %param.20) | copy-start | bytes 6148
  7.2 13.7 %copy-start.32 = (f32[2,1024]{1,0:T(2,128)S(1)}, f32[2,1024]{1,0:T(2,128)}, u32[]{:S(2)}) copy-start(f32[2,1024]{1,0:T(2,128)} %param.18) | copy-start | bytes 24580
  7.2 14.3 %copy-start.14 = (f32[2,3,3,1024]{3,0,2,1:T(2,128)S(1)}, f32[2,3,3,1024]{3,0,2,1:T(2,128)}, u32[]{:S(2)}) copy-start(f32[2,3,3,1024]{3,0,2,1:T(2,128)} %param.17) | copy-start | bytes 221188
  7.2 14.4 %copy-start.9 = (f32[2,5,5,768]{3,0,2,1:T(2,128)S(1)}, f32[2,5,5,768]{3,0,2,1:T(2,128)}, u32[]{:S(2)}) copy-start(f32[2,5,5,768]{3,0,2,1:T(2,128)} %param.22) | copy-start | bytes 460804
  7.2 625.4 %all-reduce.3.cloned.1.call-start = ((), (), s32[]{:S(2)}) async-start(), calls=%async_computation | async-start | bytes 524288 | tf_op jit(solution)/shard_map/psum | solution.py:116
  8.6 13.8 %copy-start.36 = (f32[2,256]{1,0:T(2,128)S(1)}, f32[2,256]{1,0:T(2,128)}, u32[]{:S(2)}) copy-start(f32[2,256]{1,0:T(2,128)} %param.25) | copy-start | bytes 6148
  10.1 12.8 collective-permute-start
  14.7 8.2 collective-permute-start.1
  23.0 8.6 copy-start.42
  23.0 8.6 copy-start.45
  23.1 3.9 collective-permute-start.2
  24.9 6.3 collective-permute-start.3
  33.1 6.6 copy-start.10
  34.1 7.9 collective-permute-start.4
  37.8 6.1 collective-permute-start.5
  44.0 9.3 collective-permute-start.6
  50.0 6.2 collective-permute-start.7
  53.2 3.3 copy-start.15
  53.2 3.3 copy-start.16
  53.2 3.3 copy-start.17
  53.2 3.4 copy-start.18
  53.2 3.4 copy-start.19
  53.2 3.4 copy-start.20
  53.2 3.4 copy-start.21
  53.2 3.4 copy-start.22
  53.2 3.4 copy-start.23
  53.2 3.4 copy-start.24
  53.3 3.4 copy-start.25
  53.3 3.4 copy-start.26
  53.3 3.4 copy-start.27
  53.3 3.4 copy-start.28
  53.3 3.4 copy-start.29
  53.3 3.4 copy-start.30
  53.3 3.4 copy-start.31
  60.8 1.9 copy-start
  182.4 1071.2 %all-reduce.5.cloned.1.call-start = ((), (), s32[]{:S(2)}) async-start(), calls=%async_computation.1 | async-start | bytes 524288 | tf_op jit(solution)/shard_map/psum | solution.py:116
  638.7 2.0 copy-start.11
  638.7 2.0 copy-start.39
  638.7 3.2 copy-start.34
  639.7 2.2 copy-start.41
  642.0 16.8 %copy-start.8 = (f32[5,5,768]{2,1,0:T(8,128)S(1)}, f32[5,5,768]{2,1,0:T(8,128)}, u32[]{:S(2)}) copy-start(f32[5,5,768]{2,1,0:T(8,128)} %get-tuple-element.118) | copy-start | bytes 230404
  642.4 7.0 collective-permute-start.8
  647.3 5.6 collective-permute-start.9
  649.3 14.8 %copy-start.33 = (f32[1,1024]{1,0:T(1,128)S(1)}, f32[1,1024]{1,0:T(1,128)}, u32[]{:S(2)}) copy-start(f32[1,1024]{1,0:T(1,128)} %get-tuple-element.108) | copy-start | bytes 12292
  649.3 14.8 %copy-start.38 = (f32[1,256]{1,0:T(1,128)S(1)}, f32[1,256]{1,0:T(1,128)}, u32[]{:S(2)}) copy-start(f32[1,256]{1,0:T(1,128)} %get-tuple-element.114) | copy-start | bytes 3076
  649.3 14.8 %copy-start.43 = (bf16[2,1024,256]{2,1,0:T(8,128)(2,1)S(1)}, bf16[2,1024,256]{2,1,0:T(8,128)(2,1)}, u32[]{:S(2)}) copy-start(bf16[2,1024,256]{2,1,0:T(8,128)(2,1)} %param.19) | copy-start | bytes 3145732
  653.0 6.0 collective-permute-start.10
  657.5 6.3 collective-permute-start.11
  665.6 5.0 copy-start.12
  666.0 6.3 collective-permute-start.12
  668.7 5.9 collective-permute-start.13
  674.7 6.6 collective-permute-start.14
  677.8 6.2 collective-permute-start.15
  688.4 1.9 copy-start.2
  1259.7 2.0 copy-start.13
  1259.8 2.0 copy-start.37
  1259.8 2.0 copy-start.44
  1259.8 9.2 copy-start.40
  1261.8 21.8 %copy-start.46 = (f32[4]{0:T(128)S(1)}, f32[4]{0:T(128)}, u32[]{:S(2)}) copy-start(f32[4]{0:T(128)} %param.27) | copy-start | bytes 52
  1262.0 22.4 %copy-start.4 = (bf16[8,32,256]{2,1,0:T(8,128)(2,1)}, bf16[8,32,256]{2,1,0:T(8,128)(2,1)S(1)}, u32[]{:S(2)}) copy-start(bf16[8,32,256]{2,1,0:T(8,128)(2,1)S(1)} %fusion.9) | copy-start | bytes 393220
  1262.1 7.1 collective-permute-start.16
  1267.0 5.1 collective-permute-start.17
  1272.1 6.2 collective-permute-start.18
  1276.6 5.9 collective-permute-start.19
  (5 other events, 7.0 us)
Sparse Core Ops, SparseCore 0:
  182.6 449.9 all-reduce.2
  805.0 448.5 all-reduce.4
where the time goes:
time: 1290 us
  waiting for transfers between devices  929 us (72%)
  blocking collectives  217 us (17%)
  starting transfers between devices  60.7 us (5%)
  matrix products  35 us (3%)
  local copies, waits for them, and re-layouts  26.6 us (2%)
  between operations  15.2 us (1%)
    psum x2, waiting for transfers between devices, local(): kv_all, key_all = lax.psum((kv_local, key_local), ('row', 'col'))  899 us
    psum x2, blocking collectives, local(): kv_all, key_all = lax.psum((kv_local, key_local), ('row', 'col'))  217 us
    ppermute x10, starting transfers between devices, with_halo(): lax.ppermute(tail, axis, [(i, (i + 1) % count) for i in range(ends)])  40.8 us
    ppermute x10, waiting for transfers between devices, with_halo(): lax.ppermute(head, axis, [((i + 1) % count, i) for i in range(ends)])  29.7 us
  transfers between devices with their start and end apart: 22, of which 11 were waited for; matrix products, arithmetic and copies ran while one was open for 1% of the time, Pallas kernels for 0%

commit v1 on v0

--- a/solution.py
+++ b/solution.py
@@ -113,7 +113,7 @@
         values = both[:, :, :, 2, :].astype(jnp.float32)
         kv_local = jnp.einsum("rchd,rche->hde", keys, values, precision=lax.Precision.HIGHEST)
         key_local = jnp.sum(keys, axis=(0, 1))
-        kv_all, key_all = lax.psum((kv_local, key_local), ("row", "col"))
+        kv_all, key_all = lax.psum(lax.psum((kv_local, key_local), "col"), "row")
         numer = jnp.einsum("rchd,hde->rche", queries, kv_all, precision=lax.Precision.HIGHEST)
         denom = jnp.einsum("rchd,hd->rch", queries, key_all, precision=lax.Precision.HIGHEST)
         attended = (

time: 1290 us -> 1240 us (0.961)
  waiting for transfers between devices: 929 us -> 883 us
    psum x2 -> x4, waiting for transfers between devices: 899 us -> 855 us  [local(): kv_all, key_all = lax.psum(lax.psum((kv_local, key_local), 'col'), 'row')]
    psum x2 -> x4, blocking collectives: 217 us -> 211 us  [local(): kv_all, key_all = lax.psum(lax.psum((kv_local, key_local), 'col'), 'row')]
  transfers between devices with their start and end apart: 22 -> 24, of which waited for: 11 -> 13; matrix products, arithmetic and copies ran while one was open for 1% -> 2% of each run, Pallas kernels for 0% -> 0%
where the time goes in v1:
time: 1240 us
  waiting for transfers between devices  883 us (71%)
  blocking collectives  211 us (17%)
  starting transfers between devices  58.8 us (5%)
  matrix products  35 us (3%)
  local copies, waits for them, and re-layouts  26.6 us (2%)
  between operations  15 us (1%)
    psum x4, waiting for transfers between devices, local(): kv_all, key_all = lax.psum(lax.psum((kv_local, key_local), 'col'), 'row')  855 us
    psum x4, blocking collectives, local(): kv_all, key_all = lax.psum(lax.psum((kv_local, key_local), 'col'), 'row')  211 us
    ppermute x10, starting transfers between devices, with_halo(): lax.ppermute(tail, axis, [(i, (i + 1) % count) for i in range(ends)])  36.9 us
    ppermute x10, waiting for transfers between devices, with_halo(): lax.ppermute(head, axis, [((i + 1) % count, i) for i in range(ends)])  28.3 us
  transfers between devices with their start and end apart: 24, of which 13 were waited for; matrix products, arithmetic and copies ran while one was open for 2% of the time, Pallas kernels for 0%

profile of v1, /device:TPU:1, one launch (start us, length us, event | category | flops | bytes accessed | tf_op | source)
XLA Modules:
  0.0 1238.3 jit_solution(15530430636415531474)
XLA Ops:
  7.3 1.4 fusion.129
  8.6 1.5 multiply_convert_fusion.3
  10.1 4.6 collective-permute-start
  14.7 5.5 collective-permute-start.1
  23.1 1.9 collective-permute-start.2
  24.9 1.3 collective-permute-start.3
  27.0 4.2 collective-permute-done.3
  31.6 1.5 fusion.11
  34.1 3.7 collective-permute-start.4
  37.8 1.9 collective-permute-start.5
  40.4 1.6 reshape.49
  42.0 2.0 collective-permute-done.5
  44.0 6.0 collective-permute-start.6
  50.0 1.3 collective-permute-start.7
  51.3 1.9 copy_dynamic-update-slice_fusion.3
  53.3 2.9 collective-permute-done.7
  56.7 3.0 add_convert_fusion.1
  59.7 1.1 reshape.50
  61.3 1.3 copy-done
  63.4 1.4 copy-done.1
  64.8 1.1 convolution_bitcast_fusion.1
  66.0 67.0 %psum.58 = f32[16,32]{1,0:T(8,128)S(1)} all-reduce(f32[16,32]{1,0:T(8,128)S(1)} %convert_reduce_fusion.1), channel_id=1, replica_groups=mesh['row'=16,'col'=32] {'col'}, use_global_device_ids=true, to_apply=%region_3.4 | all-reduce | flops 512 | bytes 4096 | tf_op jit(solution)/shard_map/psum | solution.py:116
  133.0 41.1 %psum.59 = f32[16,32]{1,0:T(8,128)S(1)} all-reduce(f32[16,32]{1,0:T(8,128)S(1)} %psum.58), channel_id=1, replica_groups=mesh['row'=16,'col'=32] {'row'}, use_global_device_ids=true, to_apply=%region_4.5 | all-reduce | flops 512 | bytes 4096 | tf_op jit(solution)/shard_map/psum | solution.py:116
  174.3 5.4 fusion.26
  179.7 276.1 %all-reduce.5.cloned.1.call-done = f32[16,32,32]{1,2,0:T(8,128)} async-done(((f32[16,32,32]{1,2,0:T(8,128)}), f32[16,32,32]{1,2,0:T(8,128)}) %all-reduce.5.cloned.1.call-update) | async-done | bytes 65552 | tf_op jit(solution)/shard_map/psum | solution.py:116
  455.8 150.4 %all-reduce.7.cloned.1.call-done = f32[16,32,32]{1,2,0:T(8,128)} async-done(((f32[16,32,32]{1,2,0:T(8,128)}), f32[16,32,32]{1,2,0:T(8,128)}) %all-reduce.7.cloned.1.call-update) | async-done | bytes 65552 | tf_op jit(solution)/shard_map/psum | solution.py:116
  606.2 6.1 fusion.1
  612.4 1.0 copy.25
  613.4 1.0 reshape.52
  614.4 1.2 fusion.8
  616.0 1.9 collective-permute-start.8
  617.9 2.6 collective-permute-start.9
  620.7 2.9 collective-permute-done.9
  623.6 4.4 collective-permute-start.10
  628.0 1.3 collective-permute-start.11
  629.4 4.8 collective-permute-done.11
  634.6 1.5 fusion.10
  636.5 2.7 collective-permute-start.12
  639.2 1.9 collective-permute-start.13
  641.2 1.6 reshape.53
  642.8 2.3 collective-permute-done.13
  645.2 5.5 collective-permute-start.14
  650.7 1.5 collective-permute-start.15
  652.2 1.9 copy_dynamic-update-slice_fusion.1
  654.1 2.8 collective-permute-done.15
  657.2 3.0 add_convert_fusion
  660.2 1.1 reshape.54
  661.9 1.3 copy-done.2
  664.0 1.4 copy-done.3
  665.3 1.1 convolution_bitcast_fusion
  666.5 62.0 %psum.62 = f32[16,32]{1,0:T(8,128)S(1)} all-reduce(f32[16,32]{1,0:T(8,128)S(1)} %convert_reduce_fusion), channel_id=1, replica_groups=mesh['row'=16,'col'=32] {'col'}, use_global_device_ids=true, to_apply=%region_8.9 | all-reduce | flops 512 | bytes 4096 | tf_op jit(solution)/shard_map/psum | solution.py:116
  728.5 41.4 %psum.63 = f32[16,32]{1,0:T(8,128)S(1)} all-reduce(f32[16,32]{1,0:T(8,128)S(1)} %psum.62), channel_id=1, replica_groups=mesh['row'=16,'col'=32] {'row'}, use_global_device_ids=true, to_apply=%region_9.10 | all-reduce | flops 512 | bytes 4096 | tf_op jit(solution)/shard_map/psum | solution.py:116
  770.2 5.4 fusion.29
  775.6 278.1 %all-reduce.9.cloned.1.call-done = f32[16,32,32]{1,2,0:T(8,128)} async-done(((f32[16,32,32]{1,2,0:T(8,128)}), f32[16,32,32]{1,2,0:T(8,128)}) %all-reduce.9.cloned.1.call-update) | async-done | bytes 65552 | tf_op jit(solution)/shard_map/psum | solution.py:116
  1053.7 150.3 %all-reduce.11.cloned.1.call-done = f32[16,32,32]{1,2,0:T(8,128)} async-done(((f32[16,32,32]{1,2,0:T(8,128)}), f32[16,32,32]{1,2,0:T(8,128)}) %all-reduce.11.cloned.1.call-update) | async-done | bytes 65552 | tf_op jit(solution)/shard_map/psum | solution.py:116
  1204.0 6.1 fusion
  1210.2 1.0 copy.31
  1211.2 1.0 reshape.56
  1212.5 1.9 collective-permute-start.16
  1214.4 2.6 collective-permute-start.17
  1217.3 2.2 collective-permute-done.17
  1219.5 4.4 collective-permute-start.18
  1223.9 1.3 collective-permute-start.19
  1225.6 4.2 collective-permute-done.19
  (159 shorter events, 13.8 us)
Async XLA Ops:
  7.2 13.1 %copy-start.35 = (f32[2,256]{1,0:T(2,128)S(1)}, f32[2,256]{1,0:T(2,128)}, u32[]{:S(2)}) copy-start(f32[2,256]{1,0:T(2,128)} %param.20) | copy-start | bytes 6148
  7.2 13.7 %copy-start.32 = (f32[2,1024]{1,0:T(2,128)S(1)}, f32[2,1024]{1,0:T(2,128)}, u32[]{:S(2)}) copy-start(f32[2,1024]{1,0:T(2,128)} %param.18) | copy-start | bytes 24580
  7.2 14.3 %copy-start.14 = (f32[2,3,3,1024]{3,0,2,1:T(2,128)S(1)}, f32[2,3,3,1024]{3,0,2,1:T(2,128)}, u32[]{:S(2)}) copy-start(f32[2,3,3,1024]{3,0,2,1:T(2,128)} %param.17) | copy-start | bytes 221188
  7.2 14.4 %copy-start.9 = (f32[2,5,5,768]{3,0,2,1:T(2,128)S(1)}, f32[2,5,5,768]{3,0,2,1:T(2,128)}, u32[]{:S(2)}) copy-start(f32[2,5,5,768]{3,0,2,1:T(2,128)} %param.22) | copy-start | bytes 460804
  7.2 448.5 %all-reduce.5.cloned.1.call-start = ((), (), s32[]{:S(2)}) async-start(), calls=%async_computation | async-start | bytes 524288 | tf_op jit(solution)/shard_map/psum | solution.py:116
  8.6 13.8 %copy-start.36 = (f32[2,256]{1,0:T(2,128)S(1)}, f32[2,256]{1,0:T(2,128)}, u32[]{:S(2)}) copy-start(f32[2,256]{1,0:T(2,128)} %param.25) | copy-start | bytes 6148
  10.1 12.8 %collective-permute-start = (bf16[1,32,1024]{2,1,0:T(8,128)(2,1)S(1)}, bf16[1,32,1024]{2,1,0:T(8,128)(2,1)S(1)}, u32[]{:S(2)}, u32[]{:S(2)}) collective-permute-start(bf16[1,32,1024]{2,1,0:T(8,128)(2,1)S(1)} %get-tuple-element.74), channel_id=1, source_target_pairs={{0,32},{32,64},{64,96},{96,128},{128,160},{160,192},{192,224},{224... | collective-permute-start | bytes 196616 | tf_op jit(solution)/shard_map/ppermute | solution.py:17
  14.7 8.2 collective-permute-start.1
  23.0 8.6 copy-start.42
  23.0 8.6 copy-start.45
  23.1 3.9 collective-permute-start.2
  24.9 6.3 collective-permute-start.3
  33.1 6.6 copy-start.10
  34.1 7.9 collective-permute-start.4
  37.8 6.1 collective-permute-start.5
  44.0 9.3 collective-permute-start.6
  50.0 6.2 collective-permute-start.7
  53.2 3.3 copy-start.15
  53.2 3.3 copy-start.16
  53.2 3.3 copy-start.17
  53.2 3.4 copy-start.18
  53.2 3.4 copy-start.19
  53.2 3.4 copy-start.20
  53.2 3.4 copy-start.21
  53.2 3.4 copy-start.22
  53.2 3.4 copy-start.23
  53.2 3.4 copy-start.24
  53.3 3.4 copy-start.25
  53.3 3.4 copy-start.26
  53.3 3.4 copy-start.27
  53.3 3.4 copy-start.28
  53.3 3.4 copy-start.29
  53.3 3.4 copy-start.30
  53.3 3.4 copy-start.31
  174.1 432.1 %all-reduce.7.cloned.1.call-start = ((), (), s32[]{:S(2)}) async-start(), calls=%async_computation.1 | async-start | bytes 524288 | tf_op jit(solution)/shard_map/psum | solution.py:116
  455.8 597.9 %all-reduce.9.cloned.1.call-start = ((), (), s32[]{:S(2)}) async-start(), calls=%async_computation.2 | async-start | bytes 524288 | tf_op jit(solution)/shard_map/psum | solution.py:116
  612.4 2.0 copy-start.11
  612.4 2.0 copy-start.39
  612.4 3.2 copy-start.34
  613.4 2.2 copy-start.41
  615.6 13.6 %copy-start.8 = (f32[5,5,768]{2,1,0:T(8,128)S(1)}, f32[5,5,768]{2,1,0:T(8,128)}, u32[]{:S(2)}) copy-start(f32[5,5,768]{2,1,0:T(8,128)} %get-tuple-element.118) | copy-start | bytes 230404
  616.0 4.6 collective-permute-start.8
  617.9 5.6 collective-permute-start.9
  620.6 13.9 %copy-start.33 = (f32[1,1024]{1,0:T(1,128)S(1)}, f32[1,1024]{1,0:T(1,128)}, u32[]{:S(2)}) copy-start(f32[1,1024]{1,0:T(1,128)} %get-tuple-element.108) | copy-start | bytes 12292
  620.6 13.9 %copy-start.38 = (f32[1,256]{1,0:T(1,128)S(1)}, f32[1,256]{1,0:T(1,128)}, u32[]{:S(2)}) copy-start(f32[1,256]{1,0:T(1,128)} %get-tuple-element.114) | copy-start | bytes 3076
  620.6 13.9 %copy-start.43 = (bf16[2,1024,256]{2,1,0:T(8,128)(2,1)S(1)}, bf16[2,1024,256]{2,1,0:T(8,128)(2,1)}, u32[]{:S(2)}) copy-start(bf16[2,1024,256]{2,1,0:T(8,128)(2,1)} %param.19) | copy-start | bytes 3145732
  623.6 5.8 collective-permute-start.10
  628.0 6.3 collective-permute-start.11
  636.1 5.0 copy-start.12
  636.5 6.3 collective-permute-start.12
  639.2 5.9 collective-permute-start.13
  645.2 9.0 collective-permute-start.14
  650.7 6.2 collective-permute-start.15
  769.9 434.1 %all-reduce.11.cloned.1.call-start = ((), (), s32[]{:S(2)}) async-start(), calls=%async_computation.3 | async-start | bytes 524288 | tf_op jit(solution)/shard_map/psum | solution.py:116
  1210.2 2.0 copy-start.13
  1210.2 2.0 copy-start.37
  1210.2 2.0 copy-start.44
  1210.2 6.9 copy-start.40
  1212.2 18.6 %copy-start.46 = (f32[4]{0:T(128)S(1)}, f32[4]{0:T(128)}, u32[]{:S(2)}) copy-start(f32[4]{0:T(128)} %param.27) | copy-start | bytes 52
  1212.5 19.2 %copy-start.4 = (bf16[8,32,256]{2,1,0:T(8,128)(2,1)}, bf16[8,32,256]{2,1,0:T(8,128)(2,1)S(1)}, u32[]{:S(2)}) copy-start(bf16[8,32,256]{2,1,0:T(8,128)(2,1)S(1)} %fusion.9) | copy-start | bytes 393220
  1212.5 4.8 collective-permute-start.16
  1214.4 5.1 collective-permute-start.17
  1219.5 6.0 collective-permute-start.18
  1223.9 5.9 collective-permute-start.19
  (7 other events, 10.8 us)
Sparse Core Ops, SparseCore 0:
  174.2 281.4 all-reduce.4
  458.9 147.2 all-reduce.6
  770.1 283.6 all-reduce.8
  1056.7 147.2 all-reduce.10
